TPU v7x, 1024 devices: a whole 4x8x16 slice. The times are simulated.
1024 devices in a mesh: fsdp: 64 (over y, x, core), expert: 16 (over z).
Axes of the slice: x: 4, y: 8, z: 16, core: 2. Of those that a mesh axis runs over, the one named last changes fastest.
Arguments:
- deltas: bfloat16 [1024, 128, 128], P(('fsdp', 'expert')), may hold values from -6 to 6
- scales: bfloat16 [1024], P(('fsdp', 'expert')), may hold values from 0.049804688 to 0.5
- held_block: int32 [1024], P(('fsdp', 'expert')), may hold values from -1 to 223, as said below
- block_dest: int32 [224], replicated, may hold values from 0 to 447, as said below
- rollout_old: bfloat16 [448, 128, 128], P('expert'), may hold values from -6 to 6
Outputs:
- rollout_new: bfloat16 [448, 128, 128], P('expert')
Inputs may be any that keep to these rules, and one draw needn't show every extreme that they name: `held_block`: each of the 224 block numbers stands in exactly one slot, -1 in the others; a trainer device holds at most 1 block. `block_dest`: distinct values; a slot's owner is its value // 28. Some owner receives exactly 28 blocks. The blocks held by the trainer devices of one expert index and destined to one owner number at most 2, and some such pair reaches 2.
All inputs are finite; a program needn't handle non-finite values.
Results may differ from a plain program's by a relative error of at most 0.001.
Values may be sent and summed in bfloat16 or wider, within the bound.
A program may use at most 32 MiB of HBM per device.

v0:
```python
import jax
import jax.numpy as jnp
from jax import lax
from jax.sharding import PartitionSpec as P


def locate(held_part, block_dest):
    numbers = jnp.arange(block_dest.shape[0], dtype=jnp.int32)
    matches = held_part[:, None] == numbers[None, :]
    target = jnp.sum(jnp.where(matches, block_dest[None, :], 0), axis=1)
    return (target, held_part >= 0)


def pack_slots(carry, piece, block_dest, capacity, owner_count, pair_depth):
    send_values, send_scales, send_target, counts = carry
    values, scale_part, held_part = piece
    target, is_valid = locate(held_part, block_dest)
    owner_of = jnp.where(is_valid, target // capacity, 0)
    onehot = (
        (owner_of[:, None] == jnp.arange(owner_count, dtype=jnp.int32)[None, :]) & is_valid[:, None]
    ).astype(jnp.int32)
    before = jnp.cumsum(onehot, axis=0) - onehot
    position = jnp.sum(before * onehot, axis=1)
    dest_index = jnp.where(is_valid, owner_of * pair_depth + position, owner_count * pair_depth)
    send_values = send_values.at[dest_index].set(values, mode="drop")
    send_scales = send_scales.at[dest_index].set(scale_part, mode="drop")
    send_target = send_target.at[dest_index].set(target, mode="drop")
    counts = jnp.sum(onehot, axis=0)
    return (send_values, send_scales, send_target, counts)


def blank_buffers(owner_count, depth, block_size):
    rows_total = owner_count * depth
    return (
        jnp.zeros((rows_total, block_size, block_size), jnp.bfloat16),
        jnp.zeros((rows_total,), jnp.bfloat16),
        jnp.full((rows_total,), -1, jnp.int32),
        jnp.zeros((owner_count,), jnp.int32),
    )


def shards(deltas, scales, held_block, block_dest, rollout_old):
    owner_count = lax.axis_size("expert")
    capacity = rollout_old.shape[0]
    block_size = rollout_old.shape[1]
    pair_depth = (capacity + owner_count - 1) // owner_count
    buffer_rows = owner_count * pair_depth
    blank_state = blank_buffers(owner_count, pair_depth, block_size)
    gathered = (
        lax.all_gather(deltas, "fsdp", axis=0, tiled=True),
        lax.all_gather(scales, "fsdp", axis=0, tiled=True),
        lax.all_gather(held_block, "fsdp", axis=0, tiled=True),
    )
    packed = pack_slots(blank_state, gathered, block_dest, capacity, owner_count, pair_depth)
    send_values, send_scales, send_target, unused_counts = packed
    routed = (
        lax.all_to_all(
            send_values.reshape(owner_count, pair_depth, block_size, block_size),
            "expert",
            split_axis=0,
            concat_axis=0,
            tiled=True,
        ),
        lax.all_to_all(
            send_scales.reshape(owner_count, pair_depth),
            "expert",
            split_axis=0,
            concat_axis=0,
            tiled=True,
        ),
        lax.all_to_all(
            send_target.reshape(owner_count, pair_depth),
            "expert",
            split_axis=0,
            concat_axis=0,
            tiled=True,
        ),
    )
    recv_values = routed[0].reshape(buffer_rows, block_size, block_size)
    recv_scales = routed[1].reshape(buffer_rows)
    recv_target = routed[2].reshape(buffer_rows)
    local_slot = jnp.where(recv_target >= 0, recv_target % capacity, capacity).astype(jnp.int32)
    update = recv_values.astype(jnp.float32) * recv_scales.astype(jnp.float32)[:, None, None]
    added_sum = (
        jnp.zeros((capacity, block_size, block_size), jnp.float32)
        .at[local_slot]
        .add(update, mode="drop")
    )
    return (rollout_old.astype(jnp.float32) + added_sum).astype(jnp.bfloat16)


def solution(mesh):
    in_specs = (
        P(("fsdp", "expert"), None, None),
        P(("fsdp", "expert")),
        P(("fsdp", "expert")),
        P(),
        P("expert", None, None),
    )
    out_specs = P("expert", None, None)
    return jax.shard_map(shards, mesh=mesh, in_specs=in_specs, out_specs=out_specs, check_vma=False)
```

profile of v0, /device:TPU:1, one launch (start us, length us, event | category | flops | bytes accessed | tf_op | source)
XLA Modules:
  0.0 275.5 jit_solution(5152812634156254324)
XLA Ops:
  6.5 0.0 all-gather.2.cloned.1.call-start
  6.5 0.7 all-gather.2.cloned.1.call-update
  8.6 1.3 dynamic-slice
  9.8 0.8 dynamic-update-slice
  10.6 18.3 %all-reduce = s32[64]{0:T(128)S(1)} all-reduce(s32[64]{0:T(128)S(1)} %dynamic-update-slice), channel_id=1, replica_groups=mesh['fsdp'=64,'expert'=16] {'fsdp'}, use_global_device_ids=true, to_apply=%add | all-reduce | flops 64 | bytes 512
  28.9 0.9 select_reduce_fusion
  29.8 0.1 fusion.1
  29.9 0.1 reduce_window_sum.11
  30.0 0.8 dynamic-update-slice.1
  30.7 135.5 %all-reduce.1 = bf16[64]{0:T(256)(128)(2,1)S(1)} all-reduce(bf16[64]{0:T(256)(128)(2,1)S(1)} %dynamic-update-slice.1), channel_id=1, replica_groups=mesh['fsdp'=64,'expert'=16] {'fsdp'}, use_global_device_ids=true, to_apply=%add.1 | all-reduce | flops 64 | bytes 256
  166.3 0.2 select_reduce_fusion.1
  166.4 1.0 scatter_custom_fusion.2
  167.4 0.7 all_to_all.20
  168.1 11.3 %all-to-all-start.2 = ((bf16[16,1,2]{2,1,0:T(2,128)(2,1)}), bf16[16,1,2]{2,1,0:T(2,128)(2,1)S(1)}, u32[]{:S(2)}, u32[]{:S(2)}) async-start(bf16[16,1,2]{2,1,0:T(2,128)(2,1)} %all_to_all.20), calls=%async_computation.2 | async-start | bytes 16384 | tf_op jit(solution)/shard_map/all_to_all | solution.py:64
  179.4 0.8 scatter_custom_fusion
  180.2 0.7 all_to_all.15
  180.9 9.8 %all-to-all-done.2 = bf16[16,1,2]{2,1,0:T(2,128)(2,1)S(1)} async-done(((bf16[16,1,2]{2,1,0:T(2,128)(2,1)}), bf16[16,1,2]{2,1,0:T(2,128)(2,1)S(1)}, u32[]{:S(2)}, u32[]{:S(2)}) %all-to-all-start.2) | async-done | bytes 96 | tf_op jit(solution)/shard_map/all_to_all | solution.py:64
  190.6 3.5 %all-to-all-start = ((s32[16,1,2]{2,1,0:T(1,128)}), s32[16,1,2]{2,1,0:T(1,128)S(1)}, u32[]{:S(2)}, u32[]{:S(2)}) async-start(s32[16,1,2]{2,1,0:T(1,128)} %bitcast.1), calls=%async_computation | async-start | bytes 16384 | tf_op jit(solution)/shard_map/all_to_all | solution.py:71
  194.1 0.0 all-gather.2.cloned.1.call-done
  194.1 1.2 broadcast_in_dim.47
  195.4 9.9 %scatter_fusion = bf16[32,128,128]{2,1,0:T(8,128)(2,1)} fusion(bf16[32,128,128]{2,1,0:T(8,128)(2,1)} %broadcast_in_dim.47, s32[64]{0:T(128)S(1)} %compare_select_fusion.1, bf16[64,128,128]{2,1,0:T(8,128)(2,1)} %all-gather.2.cloned.1.call-done), kind=kCustom, calls=%fused_computation.1 | custom fusion | bytes 6291712 | tf_op jit(solution)/shard_map/scatter | solution.py:25
  205.2 0.0 all-to-all-done
  205.2 11.4 %all-to-all-start.1 = ((bf16[16,2,128,128]{3,2,1,0:T(8,128)(2,1)}), bf16[16,2,128,128]{3,2,1,0:T(8,128)(2,1)S(1)}, u32[]{:S(2)}, u32[]{:S(2)}) async-start(bf16[16,2,128,128]{3,2,1,0:T(8,128)(2,1)} %bitcast.3), calls=%async_computation.1 | async-start | bytes 2097152 | tf_op jit(solution)/shard_map/all_to_all | solution.py:57
  216.6 1.4 convert_element_type.25
  218.0 0.1 reshape.81
  218.2 0.1 ge.18
  218.3 0.1 remainder_reduce_fusion
  218.3 0.1 rem.32
  218.4 42.8 %all-to-all-done.1 = bf16[16,2,128,128]{3,2,1,0:T(8,128)(2,1)S(1)} async-done(((bf16[16,2,128,128]{3,2,1,0:T(8,128)(2,1)}), bf16[16,2,128,128]{3,2,1,0:T(8,128)(2,1)S(1)}, u32[]{:S(2)}, u32[]{:S(2)}) %all-to-all-start.1) | async-done | bytes 1048608 | tf_op jit(solution)/shard_map/all_to_all | solution.py:57
  261.3 1.6 convert_multiply_fusion
  262.9 4.7 %scatter_fusion.1 = f32[28,128,128]{2,1,0:T(8,128)S(1)} fusion(f32[28,128,128]{2,1,0:T(8,128)S(1)} %convert_element_type.25, s32[32]{0:T(128)S(1)} %fusion.3, f32[32,128,128]{2,1,0:T(8,128)} %convert_multiply_fusion), kind=kCustom, calls=%fused_computation.3 | custom fusion | flops 524288 | bytes 6291584 | tf_op jit(solution)/shard_map/scatter-add | solution.py:87
  267.5 1.1 convert_element_type.31
  (8 shorter events, 0.1 us)
Async XLA Ops:
  6.5 187.6 %all-gather.2.cloned.1.call-start = ((), (), s32[]{:S(2)}) async-start(), calls=%async_computation.3 | async-start | bytes 2129920 | tf_op jit(solution)/shard_map/all_gather | solution.py:50
  168.1 22.5 %all-to-all-start.2 = ((bf16[16,1,2]{2,1,0:T(2,128)(2,1)}), bf16[16,1,2]{2,1,0:T(2,128)(2,1)S(1)}, u32[]{:S(2)}, u32[]{:S(2)}) async-start(bf16[16,1,2]{2,1,0:T(2,128)(2,1)} %all_to_all.20), calls=%async_computation.2 | async-start | bytes 16384 | tf_op jit(solution)/shard_map/all_to_all | solution.py:64
  190.6 14.6 %all-to-all-start = ((s32[16,1,2]{2,1,0:T(1,128)}), s32[16,1,2]{2,1,0:T(1,128)S(1)}, u32[]{:S(2)}, u32[]{:S(2)}) async-start(s32[16,1,2]{2,1,0:T(1,128)} %bitcast.1), calls=%async_computation | async-start | bytes 16384 | tf_op jit(solution)/shard_map/all_to_all | solution.py:71
  205.2 56.0 %all-to-all-start.1 = ((bf16[16,2,128,128]{3,2,1,0:T(8,128)(2,1)}), bf16[16,2,128,128]{3,2,1,0:T(8,128)(2,1)S(1)}, u32[]{:S(2)}, u32[]{:S(2)}) async-start(bf16[16,2,128,128]{3,2,1,0:T(8,128)(2,1)} %bitcast.3), calls=%async_computation.1 | async-start | bytes 2097152 | tf_op jit(solution)/shard_map/all_to_all | solution.py:57
Sparse Core Ops, SparseCore 0:
  11.9 102.2 all-gather.1
where the time goes:
time: 280 us; the launch traced here: 275 us
  blocking collectives  154 us (55%)
  waiting for transfers between devices  53.3 us (19%)
  starting transfers between devices  26.1 us (9%)
  local copies, waits for them, and re-layouts  17.3 us (6%)
  between operations  14.8 us (5%)
  other arithmetic  10.1 us (4%)
    unnamed x2, blocking collectives  154 us
    all_to_all x1, waiting for transfers between devices, shards(): lax.all_to_all(send_values.reshape(owner_count, pair_depth, block_size, b...  42.8 us
    all_to_all x1, starting transfers between devices, shards(): lax.all_to_all(send_values.reshape(owner_count, pair_depth, block_size, b...  11.4 us
    all_to_all x1, starting transfers between devices, shards(): lax.all_to_all(send_scales.reshape(owner_count, pair_depth), 'expert', sp...  11.3 us
    scatter x1, local copies, waits for them, and re-layouts, pack_slots(): send_values = send_values.at[dest_index].set(values, mode='drop')  9.89 us
    all_to_all x1, waiting for transfers between devices, shards(): lax.all_to_all(send_scales.reshape(owner_count, pair_depth), 'expert', sp...  9.75 us
  transfers between devices with their start and end apart: 4, of which 2 were waited for; matrix products, arithmetic and copies ran while one was open for 7% of the time, Pallas kernels for 0%

commit v1 on v0

v1 whole, which is shorter than its diff:
```python
import functools

import jax
import jax.numpy as jnp
from jax import lax
from jax.experimental import pallas as pl
from jax.experimental.pallas import tpu as pltpu
from jax.sharding import PartitionSpec as P

ROWS = 16
LANES = 128
CHUNKS = 8
COLS = 8
OWNERS = 16
PAIR = 2
TILES = CHUNKS * 2 * PAIR
F32 = jnp.float32
BF16 = jnp.bfloat16


def iota(shape, dim):
    return lax.broadcasted_iota(jnp.int32, shape, dim)


def own_meta(f, capacity, scale_ref, held_ref, dest_ref):
    held = held_ref[0]
    dest = dest_ref[jnp.maximum(held, 0)]
    owner = jnp.where(held >= 0, lax.div(dest, capacity) + 1, 0).astype(F32)
    slot = jnp.where(held >= 0, lax.rem(dest, capacity) + 1, 0).astype(F32)
    scale = jnp.broadcast_to(scale_ref[...].astype(F32), (ROWS, LANES))
    row, lane = iota((ROWS, LANES), 0), iota((ROWS, LANES), 1)
    value = jnp.where(row == 0, owner, jnp.where(row == 1, slot, jnp.where(row == 2, scale, 0.0)))
    return jnp.where(lane == f, value, 0.0).astype(BF16)


def select_blocks(e, raw, sendz):
    count = raw.shape[0]
    total = jnp.sum(raw[:, 1].astype(F32), axis=0)
    owner, slot, scale = total[0:1], total[1:2], total[2:3]
    onehot = (iota((OWNERS, LANES), 0).astype(F32) + 1.0 == owner).astype(F32)
    earlier = (iota((LANES, LANES), 0) < iota((LANES, LANES), 1)).astype(F32).astype(BF16)
    before = jnp.dot(onehot.astype(BF16), earlier, preferred_element_type=F32)
    rank = jnp.sum(onehot * before, axis=0, keepdims=True)
    place = jnp.where(owner > 0.0, rank * OWNERS + owner - 1.0, -64.0)
    wide = count * ROWS
    spread = (iota((LANES, wide), 0) == iota((LANES, wide), 1) // ROWS).astype(F32).astype(BF16)
    places = jnp.dot(jnp.broadcast_to(place, (8, LANES)).astype(BF16), spread, preferred_element_type=F32)[0:1]
    target = places.astype(jnp.int32) * ROWS + iota((1, wide), 1) % ROWS
    tall = PAIR * OWNERS * ROWS
    choose = (iota((tall, wide), 0) == target).astype(F32).astype(BF16)
    data = raw[:, 0].reshape(wide, LANES)
    chosen = jnp.dot(choose, data, preferred_element_type=F32).astype(BF16).reshape(PAIR, OWNERS, ROWS, LANES)
    for k in range(PAIR):
        sendz[:, k] = chosen[k]
    mine = iota((PAIR * OWNERS, LANES), 0).astype(F32) == place
    slots = jnp.sum(jnp.where(mine, slot, 0.0), axis=1, keepdims=True)
    scales = jnp.sum(jnp.where(mine, scale, 0.0), axis=1, keepdims=True)
    lane = iota((OWNERS, LANES), 1)
    q, half = lax.rem(e, COLS), lax.div(e, COLS)
    start = lax.rem(q, 2) * 64 + half * 32
    first = (lane >= start) & (lane < start + ROWS)
    second = (lane >= start + ROWS) & (lane < start + 2 * ROWS)

    def placed(column):
        return jnp.where(first, column[:OWNERS], jnp.where(second, column[OWNERS:], 0.0))

    slots, scales = placed(slots), placed(scales)
    row = iota((ROWS, LANES), 0)
    at = 2 * lax.div(q, 2)
    for o in range(OWNERS):
        tile = jnp.where(row == at, slots[o : o + 1], jnp.where(row == at + 1, scales[o : o + 1], 0.0))
        sendz[o, 2] = tile.astype(BF16)


def kernel(
    capacity, scale_ref, held_ref, dest_ref, deltas_ref, old_ref, out_ref,
    sb, raw, sendz, zbuf, grid, old, in_sem, old_sem,
    send1, recv1, send2, recv2, send3, recv3, send4, recv4, send5, recv5,
):
    f, e = lax.axis_index("fsdp"), lax.axis_index("expert")
    r, q = lax.div(f, COLS), lax.rem(f, COLS)
    x, core = lax.div(q, 2), lax.rem(q, 2)
    plane_q, half = lax.rem(e, COLS), lax.div(e, COLS)
    collects = q == plane_q

    def remote(src, dst, send, recv, to_f, to_e):
        return pltpu.make_async_remote_copy(
            src_ref=src, dst_ref=dst, send_sem=send, recv_sem=recv,
            device_id={"fsdp": to_f, "expert": to_e}, device_id_type=pl.DeviceIdType.MESH,
        )

    def wait_bytes(ref, sem):
        pltpu.make_async_copy(ref, ref, sem).wait()

    fetch = pltpu.make_async_copy(deltas_ref, sb.at[:, 0], in_sem)
    fetch.start()
    fetch_old = pltpu.make_async_copy(old_ref, old, old_sem)
    fetch_old.start()
    meta = own_meta(f, capacity, scale_ref, held_ref, dest_ref)
    for chunk in range(CHUNKS):
        sb[chunk, 1] = meta
    fetch.wait()

    for i in range(CHUNKS):
        def send_chunk(i=i):
            remote(sb.at[i], raw.at[f], send1, recv1, i * COLS + plane_q, e).start()
        if_other = jnp.logical_not(collects & (r == i))
        pl.when(if_other)(send_chunk)

    @pl.when(collects)
    def _():
        raw[f] = sb[r]
        wait_bytes(raw.at[pl.ds(0, CHUNKS * COLS - 1)], recv1)
        select_blocks(e, raw, sendz)
        for d in range(1, OWNERS):
            to = lax.rem(e + d, OWNERS)
            remote(sendz.at[to], zbuf.at[half], send2, recv2.at[half], f, to).start()
        zbuf[half] = sendz[e]
        wait_bytes(sb.at[pl.ds(0, CHUNKS - 1)], send1)

    @pl.when(jnp.logical_not(collects))
    def _():
        wait_bytes(sb, send1)

    for h in range(2):
        def arrive(h=h):
            wait_bytes(zbuf.at[h], recv2.at[h])
        pl.when(jnp.logical_not(collects & (half == h)))(arrive)
    for h in range(2):
        for k in range(PAIR):
            grid[q, r * 4 + h * PAIR + k] = zbuf[h, k]
    grid[q, TILES] = zbuf[0, 2] + zbuf[1, 2]

    for d in range(1, CHUNKS):
        to = lax.rem(r + d, CHUNKS)
        part = grid.at[q, pl.ds(r * 4, 4)]
        remote(part, part, send3, recv3, to * COLS + q, e).start()
    wait_bytes(grid.at[q, pl.ds(0, 4 * (CHUNKS - 1))], recv3)

    for d in range(1, 4):
        to = lax.rem(x + d, 4)
        remote(grid.at[q], grid.at[q], send4, recv4.at[d - 1], r * COLS + to * 2 + core, e).start()
    sibling = r * COLS + x * 2 + (1 - core)
    remote(grid.at[q], grid.at[q], send5, recv5.at[0], sibling, e).start()
    for d in range(1, 4):
        src = lax.rem(x + 4 - d, 4) * 2 + core
        wait_bytes(grid.at[src], recv4.at[d - 1])
        remote(grid.at[src], grid.at[src], send5, recv5.at[d], sibling, e).start()
    for d in range(4):
        src = lax.rem(x + 4 - d, 4) * 2 + (1 - core)
        wait_bytes(grid.at[src], recv5.at[d])

    total = jnp.sum(grid[:, TILES].astype(F32), axis=0)
    slots = jnp.concatenate([total[2 * g : 2 * g + 1] for g in range(4)], axis=1)
    scales = jnp.concatenate([total[2 * g + 1 : 2 * g + 2] for g in range(4)], axis=1)
    deep = 4 * LANES
    target = (slots.astype(jnp.int32) - 1) * ROWS + iota((1, deep), 1) % ROWS
    tall = capacity * ROWS
    weights = jnp.where(iota((tall, deep), 0) == target, scales, 0.0).astype(BF16)
    fetch_old.wait()
    for i in range(CHUNKS):
        values = grid[:, pl.ds(i * 4, 4)].reshape(deep, LANES)
        update = jnp.dot(weights, values, preferred_element_type=F32)
        new = old[:, i].astype(F32) + update.reshape(capacity, ROWS, LANES)
        out_ref[:, i] = new.astype(BF16)

    wait_bytes(grid.at[q, pl.ds(0, 4 * (CHUNKS - 1))], send3)
    wait_bytes(grid.at[pl.ds(0, 3)], send4)
    wait_bytes(grid.at[pl.ds(0, 4)], send5)

    @pl.when(collects)
    def _():
        wait_bytes(sendz.at[pl.ds(0, OWNERS - 1)], send2)


def shards(deltas, scales, held_block, block_dest, rollout_old):
    capacity, size = rollout_old.shape[0], rollout_old.shape[1]
    count = CHUNKS * COLS
    dma, vmem = pltpu.SemaphoreType.DMA, pltpu.VMEM
    out = pl.pallas_call(
        functools.partial(kernel, capacity),
        out_shape=jax.ShapeDtypeStruct((capacity, CHUNKS, ROWS, LANES), BF16),
        in_specs=[
            pl.BlockSpec(memory_space=pltpu.VMEM),
            pl.BlockSpec(memory_space=pltpu.SMEM),
            pl.BlockSpec(memory_space=pltpu.SMEM),
            pl.BlockSpec(memory_space=pl.ANY),
            pl.BlockSpec(memory_space=pl.ANY),
        ],
        out_specs=pl.BlockSpec(memory_space=pltpu.VMEM),
        scratch_shapes=[
            vmem((CHUNKS, 2, ROWS, LANES), BF16),
            vmem((count, 2, ROWS, LANES), BF16),
            vmem((OWNERS, 3, ROWS, LANES), BF16),
            vmem((2, 3, ROWS, LANES), BF16),
            vmem((COLS, TILES + 1, ROWS, LANES), BF16),
            vmem((capacity, CHUNKS, ROWS, LANES), BF16),
            dma, dma,
            dma, dma,
            dma, dma((2,)),
            dma, dma,
            dma, dma((3,)),
            dma, dma((4,)),
        ],
        compiler_params=pltpu.CompilerParams(has_side_effects=True, vmem_limit_bytes=48 * 1024 * 1024),
    )(
        scales.reshape(1, 1),
        held_block,
        block_dest,
        deltas.reshape(CHUNKS, ROWS, LANES),
        rollout_old.reshape(capacity, CHUNKS, ROWS, LANES),
    )
    return out.reshape(capacity, size, size)


def solution(mesh):
    in_specs = (
        P(("fsdp", "expert"), None, None),
        P(("fsdp", "expert")),
        P(("fsdp", "expert")),
        P(),
        P("expert", None, None),
    )
    return jax.shard_map(shards, mesh=mesh, in_specs=in_specs, out_specs=P("expert", None, None), check_vma=False)
```

time: 280 us -> 72.9 us (0.26); the launches traced: 275 us -> 72.1 us
  blocking collectives: 154 us -> 0 us
  Pallas kernels: 0 us -> 67.2 us
  waiting for transfers between devices: 53.3 us -> 0 us
  starting transfers between devices: 26.1 us -> 0 us
  local copies, waits for them, and re-layouts: 17.3 us -> 3.53 us
  between operations: 14.8 us -> 1.32 us
  other arithmetic: 10.1 us -> 0 us
    unnamed x2 -> x0, blocking collectives: 154 us -> none
    pallas_call x0 -> x1, Pallas kernels: none -> 67.2 us  [shards(): pl.pallas_call(functools.partial(kernel, capacity), out_shape=jax.ShapeDt...]
    all_to_all x3 -> x0, waiting for transfers between devices: 52.6 us -> none  [the longest x1 42.8 us: shards(): lax.all_to_all(send_values.reshape(owner_count, pair_depth, block_size, b...]
    all_to_all x3 -> x0, starting transfers between devices: 26.1 us -> none  [the longest x1 11.4 us: shards(): lax.all_to_all(send_values.reshape(owner_count, pair_depth, block_size, b...]
    scatter x3 -> x0, local copies, waits for them, and re-layouts: 11.6 us -> none  [the longest x1 9.89 us: pack_slots(): send_values = send_values.at[dest_index].set(values, mode='drop')]
    scatter-add x1 -> x0, other arithmetic: 4.66 us -> none  [shards(): added_sum = jnp.zeros((capacity, block_size, block_size), jnp.float32).at...]
  transfers between devices with their start and end apart: 4 -> 0, of which waited for: 2 -> 0; matrix products, arithmetic and copies ran while one was open for 7% -> 0% of each run, Pallas kernels for 0% -> 0%
where the time goes in v1:
time: 72.9 us; the launch traced here: 72.1 us
  Pallas kernels  67.2 us (92%)
  local copies, waits for them, and re-layouts  3.53 us (5%)
  between operations  1.32 us (2%)
    pallas_call x1, Pallas kernels, shards(): pl.pallas_call(functools.partial(kernel, capacity), out_shape=jax.ShapeDt...  67.2 us
    unnamed x7, local copies, waits for them, and re-layouts  3.53 us

profile of v1, /device:TPU:1, one launch (start us, length us, event | category | flops | bytes accessed | tf_op | source)
XLA Modules:
  0.0 72.1 jit_solution(729283382481488028)
XLA Ops:
  1.3 0.0 copy-start.2
  1.3 0.7 copy-done.2
  2.0 0.0 copy-start
  2.0 1.2 %copy-done = bf16[28,128,128]{2,1,0:T(8,128)(2,1)S(1)} copy-done((bf16[28,128,128]{2,1,0:T(8,128)(2,1)S(1)}, bf16[28,128,128]{2,1,0:T(8,128)(2,1)}, u32[]{:S(2)}) %copy-start) | copy-done | bytes 917528
  3.2 0.0 copy-start.1
  3.2 0.8 %copy-done.1 = bf16[1,128,128]{2,1,0:T(8,128)(2,1)S(1)} copy-done((bf16[1,128,128]{2,1,0:T(8,128)(2,1)S(1)}, bf16[1,128,128]{2,1,0:T(8,128)(2,1)}, u32[]{:S(2)}) %copy-start.1) | copy-done | bytes 32792
  3.9 67.2 %shard_map.55 = bf16[28,8,16,128]{3,2,1,0:T(8,128)(2,1)S(1)} custom-call(bf16[1,1]{1,0:T(2,128)(2,1)} %bitcast.4.scale_ref, s32[1]{0:T(128)S(6)} %copy.8.held_ref, s32[224]{0:T(256)S(1)} %copy-done.2, bf16[8,16,128]{2,1,0:T(8,128)(2,1)S(1)} %bitcast.7, bf16[28,8,16,128]{3,2,1,0:T(8,128)(2,1)S(1)} %bitcast.6), custom_call_target="tpu_custom_call" | custom-call | tf_op jit(solution)/shard_map/pallas_call | solution.py:180
  71.1 0.9 %copy.9 = bf16[28,128,128]{2,1,0:T(8,128)(2,1)} copy(bf16[28,128,128]{2,1,0:T(8,128)(2,1)S(1)} %bitcast.5) | data formatting | bytes 1835008
Async XLA Ops:
  1.3 0.7 copy-start.2
  2.0 1.2 %copy-start = (bf16[28,128,128]{2,1,0:T(8,128)(2,1)S(1)}, bf16[28,128,128]{2,1,0:T(8,128)(2,1)}, u32[]{:S(2)}) copy-start(bf16[28,128,128]{2,1,0:T(8,128)(2,1)} %param.9) | copy-start | bytes 2752516
  3.2 0.8 %copy-start.1 = (bf16[1,128,128]{2,1,0:T(8,128)(2,1)S(1)}, bf16[1,128,128]{2,1,0:T(8,128)(2,1)}, u32[]{:S(2)}) copy-start(bf16[1,128,128]{2,1,0:T(8,128)(2,1)} %param.5) | copy-start | bytes 98308

commit v2 on v1

--- a/solution.py
+++ b/solution.py
@@ -27,7 +27,7 @@
     dest = dest_ref[jnp.maximum(held, 0)]
     owner = jnp.where(held >= 0, lax.div(dest, capacity) + 1, 0).astype(F32)
     slot = jnp.where(held >= 0, lax.rem(dest, capacity) + 1, 0).astype(F32)
-    scale = jnp.broadcast_to(scale_ref[...].astype(F32), (ROWS, LANES))
+    scale = jnp.broadcast_to(scale_ref[...].astype(F32).reshape(1, 1), (ROWS, LANES))
     row, lane = iota((ROWS, LANES), 0), iota((ROWS, LANES), 1)
     value = jnp.where(row == 0, owner, jnp.where(row == 1, slot, jnp.where(row == 2, scale, 0.0)))
     return jnp.where(lane == f, value, 0.0).astype(BF16)
@@ -73,8 +73,8 @@
 
 
 def kernel(
-    capacity, scale_ref, held_ref, dest_ref, deltas_ref, old_ref, out_ref,
-    sb, raw, sendz, zbuf, grid, old, in_sem, old_sem,
+    capacity, scale_hbm, held_hbm, dest_hbm, deltas_ref, old_ref, out_ref,
+    scale_ref, held_ref, dest_ref, sb, raw, sendz, zbuf, grid, old, in_sem, old_sem, small_sem,
     send1, recv1, send2, recv2, send3, recv3, send4, recv4, send5, recv5,
 ):
     f, e = lax.axis_index("fsdp"), lax.axis_index("expert")
@@ -96,10 +96,49 @@
     fetch.start()
     fetch_old = pltpu.make_async_copy(old_ref, old, old_sem)
     fetch_old.start()
+    small = [
+        pltpu.make_async_copy(src, dst, small_sem.at[i])
+        for i, (src, dst) in enumerate([(scale_hbm, scale_ref), (held_hbm, held_ref), (dest_hbm, dest_ref)])
+    ]
+    for copy in small:
+        copy.start()
+
+    barrier = pltpu.get_barrier_semaphore()
+
+    def greet(to_f, to_e):
+        pl.semaphore_signal(
+            barrier, inc=1, device_id={"fsdp": to_f, "expert": to_e}, device_id_type=pl.DeviceIdType.MESH
+        )
+
+    @pl.when(collects)
+    def _():
+        @pl.loop(1, CHUNKS * COLS)
+        def _(d):
+            greet(lax.rem(f + d, CHUNKS * COLS), e)
+
+    for h in range(2):
+        pl.when(e != q + COLS * h)(functools.partial(greet, f, q + COLS * h))
+    for d in range(1, CHUNKS):
+        greet(lax.rem(r + d, CHUNKS) * COLS + q, e)
+    for d in range(1, 4):
+        greet(r * COLS + lax.rem(x + d, 4) * 2 + core, e)
+    sibling = r * COLS + x * 2 + (1 - core)
+    greet(sibling, e)
+
+    for copy in small:
+        copy.wait()
     meta = own_meta(f, capacity, scale_ref, held_ref, dest_ref)
     for chunk in range(CHUNKS):
         sb[chunk, 1] = meta
     fetch.wait()
+
+    @pl.when(collects)
+    def _():
+        pl.semaphore_wait(barrier, 2 * (CHUNKS - 1) + OWNERS - 1 + 4)
+
+    @pl.when(jnp.logical_not(collects))
+    def _():
+        pl.semaphore_wait(barrier, CHUNKS + CHUNKS - 1 + 4)
 
     for i in range(CHUNKS):
         def send_chunk(i=i):
@@ -140,7 +179,6 @@
     for d in range(1, 4):
         to = lax.rem(x + d, 4)
         remote(grid.at[q], grid.at[q], send4, recv4.at[d - 1], r * COLS + to * 2 + core, e).start()
-    sibling = r * COLS + x * 2 + (1 - core)
     remote(grid.at[q], grid.at[q], send5, recv5.at[0], sibling, e).start()
     for d in range(1, 4):
         src = lax.rem(x + 4 - d, 4) * 2 + core
@@ -181,30 +219,33 @@
         functools.partial(kernel, capacity),
         out_shape=jax.ShapeDtypeStruct((capacity, CHUNKS, ROWS, LANES), BF16),
         in_specs=[
-            pl.BlockSpec(memory_space=pltpu.VMEM),
-            pl.BlockSpec(memory_space=pltpu.SMEM),
-            pl.BlockSpec(memory_space=pltpu.SMEM),
-            pl.BlockSpec(memory_space=pl.ANY),
-            pl.BlockSpec(memory_space=pl.ANY),
+            pl.BlockSpec(memory_space=pltpu.HBM),
+            pl.BlockSpec(memory_space=pltpu.HBM),
+            pl.BlockSpec(memory_space=pltpu.HBM),
+            pl.BlockSpec(memory_space=pltpu.HBM),
+            pl.BlockSpec(memory_space=pltpu.HBM),
         ],
         out_specs=pl.BlockSpec(memory_space=pltpu.VMEM),
         scratch_shapes=[
+            vmem((1,), BF16), pltpu.SMEM((1,), jnp.int32), pltpu.SMEM(block_dest.shape, jnp.int32),
             vmem((CHUNKS, 2, ROWS, LANES), BF16),
             vmem((count, 2, ROWS, LANES), BF16),
             vmem((OWNERS, 3, ROWS, LANES), BF16),
             vmem((2, 3, ROWS, LANES), BF16),
             vmem((COLS, TILES + 1, ROWS, LANES), BF16),
             vmem((capacity, CHUNKS, ROWS, LANES), BF16),
-            dma, dma,
+            dma, dma, dma((3,)),
             dma, dma,
             dma, dma((2,)),
             dma, dma,
             dma, dma((3,)),
             dma, dma((4,)),
         ],
-        compiler_params=pltpu.CompilerParams(has_side_effects=True, vmem_limit_bytes=48 * 1024 * 1024),
+        compiler_params=pltpu.CompilerParams(
+            collective_id=1, has_side_effects=True, vmem_limit_bytes=60 * 1024 * 1024
+        ),
     )(
-        scales.reshape(1, 1),
+        scales,
         held_block,
         block_dest,
         deltas.reshape(CHUNKS, ROWS, LANES),

time: 72.9 us -> 55.7 us (0.76)
  Pallas kernels: 67.2 us -> 52 us
  local copies, waits for them, and re-layouts: 3.53 us -> 2.2 us
    pallas_call x1, Pallas kernels: 67.2 us -> 52 us  [shards(): pl.pallas_call(functools.partial(kernel, capacity), out_shape=jax.ShapeDt...]
    unnamed x7 -> x1, local copies, waits for them, and re-layouts: 3.53 us -> 2.2 us
where the time goes in v2:
time: 55.7 us; the launch traced here: 55.5 us
  Pallas kernels  52 us (93%)
  local copies, waits for them, and re-layouts  2.2 us (4%)
  between operations  1.31 us (2%)
    pallas_call x1, Pallas kernels, shards(): pl.pallas_call(functools.partial(kernel, capacity), out_shape=jax.ShapeDt...  52 us
    unnamed x1, local copies, waits for them, and re-layouts  2.2 us

profile of v2, /device:TPU:1, one launch (start us, length us, event | category | flops | bytes accessed | tf_op | source)
XLA Modules:
  0.0 55.5 jit_solution(10523501990747323111)
XLA Ops:
  1.3 52.0 %shard_map.55 = bf16[28,8,16,128]{3,2,1,0:T(8,128)(2,1)} custom-call(bf16[1]{0:T(256)(128)(2,1)S(6)} %copy.7.scale_hbm, s32[1]{0:T(128)S(6)} %copy.8.held_hbm, s32[224]{0:T(256)} %dest_hbm.1, bf16[8,16,128]{2,1,0:T(8,128)(2,1)} %bitcast.5, bf16[28,8,16,128]{3,2,1,0:T(8,128)(2,1)} %bitcast.4), custom_call_target="tpu_custom_call" | custom-call | tf_op jit(solution)/shard_map/pallas_call | solution.py:218
  53.3 2.2 %copy.9 = bf16[28,128,128]{2,1,0:T(8,128)(2,1)} copy(bf16[28,128,128]{2,1,0:T(8,128)(2,1)} %bitcast.3) | data formatting | bytes 1835008

commit v3 on v2

--- a/solution.py
+++ b/solution.py
@@ -92,6 +92,27 @@
     def wait_bytes(ref, sem):
         pltpu.make_async_copy(ref, ref, sem).wait()
 
+    barrier = pltpu.get_barrier_semaphore()
+
+    def greet(to_f, to_e):
+        pl.semaphore_signal(
+            barrier, inc=1, device_id={"fsdp": to_f, "expert": to_e}, device_id_type=pl.DeviceIdType.MESH
+        )
+
+    @pl.when(collects)
+    def _():
+        for d in range(1, CHUNKS * COLS):
+            greet(lax.rem(f + d, CHUNKS * COLS), e)
+
+    for h in range(2):
+        pl.when(e != q + COLS * h)(functools.partial(greet, f, q + COLS * h))
+    for d in range(1, CHUNKS):
+        greet(lax.rem(r + d, CHUNKS) * COLS + q, e)
+    for d in range(1, 4):
+        greet(r * COLS + lax.rem(x + d, 4) * 2 + core, e)
+    sibling = r * COLS + x * 2 + (1 - core)
+    greet(sibling, e)
+
     fetch = pltpu.make_async_copy(deltas_ref, sb.at[:, 0], in_sem)
     fetch.start()
     fetch_old = pltpu.make_async_copy(old_ref, old, old_sem)
@@ -103,28 +124,6 @@
     for copy in small:
         copy.start()
 
-    barrier = pltpu.get_barrier_semaphore()
-
-    def greet(to_f, to_e):
-        pl.semaphore_signal(
-            barrier, inc=1, device_id={"fsdp": to_f, "expert": to_e}, device_id_type=pl.DeviceIdType.MESH
-        )
-
-    @pl.when(collects)
-    def _():
-        @pl.loop(1, CHUNKS * COLS)
-        def _(d):
-            greet(lax.rem(f + d, CHUNKS * COLS), e)
-
-    for h in range(2):
-        pl.when(e != q + COLS * h)(functools.partial(greet, f, q + COLS * h))
-    for d in range(1, CHUNKS):
-        greet(lax.rem(r + d, CHUNKS) * COLS + q, e)
-    for d in range(1, 4):
-        greet(r * COLS + lax.rem(x + d, 4) * 2 + core, e)
-    sibling = r * COLS + x * 2 + (1 - core)
-    greet(sibling, e)
-
     for copy in small:
         copy.wait()
     meta = own_meta(f, capacity, scale_ref, held_ref, dest_ref)
@@ -170,16 +169,22 @@
             grid[q, r * 4 + h * PAIR + k] = zbuf[h, k]
     grid[q, TILES] = zbuf[0, 2] + zbuf[1, 2]
 
-    for d in range(1, CHUNKS):
-        to = lax.rem(r + d, CHUNKS)
-        part = grid.at[q, pl.ds(r * 4, 4)]
-        remote(part, part, send3, recv3, to * COLS + q, e).start()
-    wait_bytes(grid.at[q, pl.ds(0, 4 * (CHUNKS - 1))], recv3)
-
-    for d in range(1, 4):
-        to = lax.rem(x + d, 4)
-        remote(grid.at[q], grid.at[q], send4, recv4.at[d - 1], r * COLS + to * 2 + core, e).start()
+    def along_x(first, count):
+        part = grid.at[q, pl.ds(first, count)]
+        for d in (2, 1, 3):
+            remote(part, part, send4, recv4.at[d - 1], r * COLS + lax.rem(x + d, 4) * 2 + core, e).start()
+
+    own = grid.at[q, pl.ds(r * 4, 4)]
+    for d in (4, 3, 5, 2, 6, 1, 7):
+        remote(own, own, send3, recv3.at[d], lax.rem(r + d, CHUNKS) * COLS + q, e).start()
+    along_x(r * 4, 4)
+    along_x(TILES, 1)
+    for d in (1, 7, 2, 6, 3, 5, 4):
+        first = lax.rem(r + CHUNKS - d, CHUNKS) * 4
+        wait_bytes(grid.at[q, pl.ds(first, 4)], recv3.at[d])
+        along_x(first, 4)
     remote(grid.at[q], grid.at[q], send5, recv5.at[0], sibling, e).start()
+
     for d in range(1, 4):
         src = lax.rem(x + 4 - d, 4) * 2 + core
         wait_bytes(grid.at[src], recv4.at[d - 1])
@@ -211,6 +216,10 @@
         wait_bytes(sendz.at[pl.ds(0, OWNERS - 1)], send2)
 
 
+def near(array):
+    return pltpu.with_memory_space_constraint(array, pltpu.HBM)
+
+
 def shards(deltas, scales, held_block, block_dest, rollout_old):
     capacity, size = rollout_old.shape[0], rollout_old.shape[1]
     count = CHUNKS * COLS
@@ -237,19 +246,19 @@
             dma, dma, dma((3,)),
             dma, dma,
             dma, dma((2,)),
-            dma, dma,
+            dma, dma((CHUNKS,)),
             dma, dma((3,)),
             dma, dma((4,)),
         ],
         compiler_params=pltpu.CompilerParams(
-            collective_id=1, has_side_effects=True, vmem_limit_bytes=60 * 1024 * 1024
+            collective_id=1, has_side_effects=True, vmem_limit_bytes=40 * 1024 * 1024
         ),
     )(
         scales,
         held_block,
-        block_dest,
-        deltas.reshape(CHUNKS, ROWS, LANES),
-        rollout_old.reshape(capacity, CHUNKS, ROWS, LANES),
+        near(block_dest),
+        near(deltas.reshape(CHUNKS, ROWS, LANES)),
+        near(rollout_old.reshape(capacity, CHUNKS, ROWS, LANES)),
     )
     return out.reshape(capacity, size, size)
 

time: 55.7 us -> 51.5 us (0.925)
  Pallas kernels: 52 us -> 49.1 us
  local copies, waits for them, and re-layouts: 2.2 us -> 0.93 us
    pallas_call x1, Pallas kernels: 52 us -> 49.1 us  [shards(): pl.pallas_call(functools.partial(kernel, capacity), out_shape=jax.ShapeDt...]
    unnamed x1, local copies, waits for them, and re-layouts: 2.2 us -> 0.93 us
where the time goes in v3:
time: 51.5 us; the launch traced here: 51.4 us
  Pallas kernels  49.1 us (95%)
  between operations  1.31 us (3%)
  local copies, waits for them, and re-layouts  0.93 us (2%)
    pallas_call x1, Pallas kernels, shards(): pl.pallas_call(functools.partial(kernel, capacity), out_shape=jax.ShapeDt...  49.1 us

profile of v3, /device:TPU:1, one launch (start us, length us, event | category | flops | bytes accessed | tf_op | source)
XLA Modules:
  0.0 51.4 jit_solution(7804147987964215300)
XLA Ops:
  1.3 49.1 %shard_map.55 = bf16[28,8,16,128]{3,2,1,0:T(8,128)(2,1)S(1)} custom-call(bf16[1]{0:T(256)(128)(2,1)S(6)} %copy.7.scale_hbm, s32[1]{0:T(128)S(6)} %copy.8.held_hbm, s32[224]{0:T(256)} %dest_hbm.1, bf16[8,16,128]{2,1,0:T(8,128)(2,1)} %bitcast.5, bf16[28,8,16,128]{3,2,1,0:T(8,128)(2,1)} %bitcast.4), custom_call_target="tpu_custom_call" | custom-call | tf_op jit(solution)/shard_map/pallas_call | solution.py:227
  50.4 0.9 %copy.9 = bf16[28,128,128]{2,1,0:T(8,128)(2,1)} copy(bf16[28,128,128]{2,1,0:T(8,128)(2,1)S(1)} %bitcast.3) | data formatting | bytes 1835008

commit v4 on v3

v4 whole, which is shorter than its diff:
```python
import functools

import jax
import jax.numpy as jnp
from jax import lax
from jax.experimental import pallas as pl
from jax.experimental.pallas import tpu as pltpu
from jax.sharding import PartitionSpec as P

ROWS = 16
LANES = 128
CHUNKS = 8
ALONG_Y = 8
OWNERS = 16
PAIR = 2
PIECE = 2 * PAIR
TILES = ALONG_Y * PIECE
FAR_FIRST = (4, 3, 5, 2, 6, 1, 7)
F32 = jnp.float32
BF16 = jnp.bfloat16


def home(e):
    return lax.rem(lax.div(e, 2) + 4, ALONG_Y)


def iota(shape, dim):
    return lax.broadcasted_iota(jnp.int32, shape, dim)


def own_meta(f, scale_ref, held_ref, dest_ref):
    held = held_ref[0]
    dest = jnp.where(held >= 0, dest_ref[jnp.maximum(held, 0)] + 1, 0).astype(F32)
    scale = jnp.broadcast_to(scale_ref[...].astype(F32).reshape(1, 1), (1, LANES))
    lane = iota((1, LANES), 1)
    return jnp.where(lane == f, dest, jnp.where(lane == f + LANES // 2, scale, 0.0))


def select_blocks(e, capacity, raw, notes, sendz):
    count = raw.shape[0]
    total = jnp.sum(notes[...], axis=0)
    scale = jnp.concatenate([total[:, LANES // 2 :], total[:, : LANES // 2]], axis=1)
    held = (iota((1, LANES), 1) < LANES // 2) & (total > 0.0)
    whole = jnp.floor((total - 0.5) * (1.0 / capacity))
    owner = jnp.where(held, whole + 1.0, 0.0)
    slot = jnp.where(held, total - whole * capacity, 0.0)
    onehot = (iota((OWNERS, LANES), 0).astype(F32) + 1.0 == owner).astype(F32)
    earlier = (iota((LANES, LANES), 0) < iota((LANES, LANES), 1)).astype(F32).astype(BF16)
    before = jnp.dot(onehot.astype(BF16), earlier, preferred_element_type=F32)
    rank = jnp.sum(onehot * before, axis=0, keepdims=True)
    place = jnp.where(owner > 0.0, rank * OWNERS + owner - 1.0, -64.0)
    wide = count * ROWS
    spread = (iota((LANES, wide), 0) == iota((LANES, wide), 1) // ROWS).astype(F32).astype(BF16)
    places = jnp.dot(jnp.broadcast_to(place, (8, LANES)).astype(BF16), spread, preferred_element_type=F32)[0:1]
    target = places.astype(jnp.int32) * ROWS + iota((1, wide), 1) % ROWS
    tall = PAIR * OWNERS * ROWS
    choose = (iota((tall, wide), 0) == target).astype(F32).astype(BF16)
    data = raw[...].reshape(wide, LANES)
    chosen = jnp.dot(choose, data, preferred_element_type=F32).astype(BF16).reshape(PAIR, OWNERS, ROWS, LANES)
    for k in range(PAIR):
        sendz[:, k] = chosen[k]
    mine = iota((PAIR * OWNERS, LANES), 0).astype(F32) == place
    slots = jnp.sum(jnp.where(mine, slot, 0.0), axis=1, keepdims=True)
    scales = jnp.sum(jnp.where(mine, scale, 0.0), axis=1, keepdims=True)
    lane = iota((OWNERS, LANES), 1)
    q, half = home(e), lax.rem(e, 2)
    start = lax.rem(q, 2) * 64 + half * 32
    first = (lane >= start) & (lane < start + ROWS)
    second = (lane >= start + ROWS) & (lane < start + 2 * ROWS)

    def placed(column):
        return jnp.where(first, column[:OWNERS], jnp.where(second, column[OWNERS:], 0.0))

    slots, scales = placed(slots), placed(scales)
    row = iota((ROWS, LANES), 0)
    at = 2 * lax.div(q, 2)
    for o in range(OWNERS):
        tile = jnp.where(row == at, slots[o : o + 1], jnp.where(row == at + 1, scales[o : o + 1], 0.0))
        sendz[o, 2] = tile.astype(BF16)


def kernel(
    capacity, scale_hbm, held_hbm, dest_hbm, deltas_ref, old_ref, out_ref,
    scale_ref, held_ref, dest_ref, sb, note, raw, notes, sendz, grid, metas, weights, old, in_sem, old_sem, small_sem,
    send1, recv1, send2, recv2, send3, recv3, send4, recv4, send5, recv5, send6, recv6, send7, recv7, send8, recv8, ready,
):
    f, e = lax.axis_index("fsdp"), lax.axis_index("expert")
    y, r = lax.div(f, CHUNKS), lax.rem(f, CHUNKS)
    x, core = lax.div(r, 2), lax.rem(r, 2)
    half = lax.rem(e, 2)
    collects = y == home(e)
    base = lax.rem(y + 4, ALONG_Y) * 2
    count = CHUNKS * ALONG_Y

    def where(to_f, to_e):
        return dict(device_id={"fsdp": to_f, "expert": to_e}, device_id_type=pl.DeviceIdType.MESH)

    def remote(src, dst, send, recv, to_f, to_e):
        return pltpu.make_async_remote_copy(
            src_ref=src, dst_ref=dst, send_sem=send, recv_sem=recv, **where(to_f, to_e)
        )

    def wait_bytes(ref, sem):
        pltpu.make_async_copy(ref, ref, sem).wait()

    barrier = pltpu.get_barrier_semaphore()

    def greet(to_f, to_e):
        pl.semaphore_signal(barrier, inc=1, **where(to_f, to_e))

    @pl.when(collects)
    def _():
        for d in range(1, count):
            greet(lax.rem(f + d, count), e)
        for plane in range(1, OWNERS):
            pl.when(plane > e)(functools.partial(greet, f, plane))

    for h in range(2):
        pl.when(e < base + h)(functools.partial(greet, f, base + h))
    for d in range(1, ALONG_Y):
        greet(lax.rem(f + d * CHUNKS, count), e)
    for d in range(1, 4):
        greet(y * CHUNKS + lax.rem(r + 2 * d, CHUNKS), e)
    sibling = y * CHUNKS + x * 2 + (1 - core)
    greet(sibling, e)

    fetch = pltpu.make_async_copy(deltas_ref, sb, in_sem)
    fetch.start()
    fetch_old = pltpu.make_async_copy(old_ref, old, old_sem)
    fetch_old.start()
    small = [
        pltpu.make_async_copy(src, dst, small_sem.at[i])
        for i, (src, dst) in enumerate([(scale_hbm, scale_ref), (held_hbm, held_ref), (dest_hbm, dest_ref)])
    ]
    for copy in small:
        copy.start()
    for copy in small:
        copy.wait()
    note[...] = own_meta(f, scale_ref, held_ref, dest_ref)
    fetch.wait()

    lower = (base < e).astype(jnp.int32) + (base + 1 < e).astype(jnp.int32)
    pl.semaphore_wait(barrier, ALONG_Y + 3 + lower + jnp.where(collects, CHUNKS - 1 + e, CHUNKS))
    for h in range(2):
        def answer(h=h):
            pl.semaphore_signal(ready, inc=1, **where(f, base + h))
        pl.when(base + h < e)(answer)

    for i in range(CHUNKS):
        def send_chunk(i=i):
            remote(sb.at[i], raw.at[f], send1, recv1, home(e) * CHUNKS + i, e).start()
            remote(note, notes.at[f], send8, recv8, home(e) * CHUNKS + i, e).start()
        pl.when(jnp.logical_not(collects & (r == i)))(send_chunk)

    @pl.when(collects)
    def _():
        raw[f] = sb[r]
        notes[f] = note[...]
        wait_bytes(raw.at[pl.ds(0, count - 1)], recv1)
        wait_bytes(notes.at[pl.ds(0, count - 1)], recv8)
        select_blocks(e, capacity, raw, notes, sendz)
        mine = pl.ds(y * PIECE + half * PAIR, PAIR)
        place = y * 2 + half

        def along_z(plane):
            remote(sendz.at[plane, pl.ds(0, PAIR)], grid.at[r, mine], send2, recv2.at[half], f, plane).start()
            remote(sendz.at[plane, PAIR], metas.at[place], send3, recv3.at[half], f, plane).start()

        for plane in range(OWNERS - 1):
            pl.when(plane < e)(functools.partial(along_z, plane))
        grid[r, mine] = sendz[e, pl.ds(0, PAIR)]
        metas[place] = sendz[e, PAIR]
        pl.when(e < OWNERS - 1)(lambda: pl.semaphore_wait(ready, OWNERS - 1 - e))
        for plane in range(1, OWNERS):
            pl.when(plane > e)(functools.partial(along_z, plane))

    def along_x(row):
        part = grid.at[r, pl.ds(row * PIECE, PIECE)]
        for d in (2, 1, 3):
            remote(part, part, send5, recv5.at[d - 1], y * CHUNKS + lax.rem(r + 2 * d, CHUNKS), e).start()

    def own_piece():
        for h in range(2):
            def arrive(h=h):
                wait_bytes(grid.at[r, pl.ds(y * PIECE + h * PAIR, PAIR)], recv2.at[h])
                wait_bytes(metas.at[y * 2 + h], recv3.at[h])
            pl.when(jnp.logical_not(collects & (half == h)))(arrive)
        part, both = grid.at[r, pl.ds(y * PIECE, PIECE)], metas.at[pl.ds(y * 2, 2)]
        for d in FAR_FIRST:
            remote(part, part, send4, recv4.at[y], lax.rem(f + d * CHUNKS, count), e).start()
        along_x(y)
        for d in FAR_FIRST:
            remote(both, both, send7, recv7, lax.rem(f + d * CHUNKS, count), e).start()

    def other_piece(row):
        def arrive():
            wait_bytes(grid.at[r, pl.ds(row * PIECE, PIECE)], recv4.at[row])
            along_x(row)
        pl.when(y != row)(arrive)

    pl.when(y >= 4)(own_piece)
    for row in range(4, 8):
        other_piece(row)
    pl.when(y < 4)(own_piece)
    for row in range(4):
        other_piece(row)

    remote(grid.at[r], grid.at[r], send6, recv6.at[0], sibling, e).start()
    wait_bytes(metas.at[pl.ds(0, 2 * (ALONG_Y - 1))], recv7)
    total = jnp.sum(metas[...].astype(F32), axis=0)
    slots = jnp.concatenate([total[2 * g : 2 * g + 1] for g in range(4)], axis=1)
    scales = jnp.concatenate([total[2 * g + 1 : 2 * g + 2] for g in range(4)], axis=1)
    deep = 4 * LANES
    target = (slots.astype(jnp.int32) - 1) * ROWS + iota((1, deep), 1) % ROWS
    tall = capacity * ROWS
    weights[...] = jnp.where(iota((tall, deep), 0) == target, scales, 0.0).astype(BF16)
    fetch_old.wait()

    def add(i):
        values = grid[i].reshape(deep, LANES)
        update = jnp.dot(weights[...], values, preferred_element_type=F32)
        new = old[:, i].astype(F32) + update.reshape(capacity, ROWS, LANES)
        out_ref[:, i] = new.astype(BF16)

    for d in (1, 3, 2):
        src = lax.rem(r + CHUNKS - 2 * d, CHUNKS)
        wait_bytes(grid.at[src], recv5.at[d - 1])
        remote(grid.at[src], grid.at[src], send6, recv6.at[d], sibling, e).start()
    for d in range(4):
        add(lax.rem(r + CHUNKS - 2 * d, CHUNKS))
    for d in (0, 1, 3, 2):
        src = lax.rem(r + CHUNKS - 2 * d, CHUNKS) + 1 - 2 * core
        wait_bytes(grid.at[src], recv6.at[d])
        add(src)

    wait_bytes(grid.at[r, pl.ds(0, PIECE * (ALONG_Y - 1))], send4)
    wait_bytes(metas.at[pl.ds(0, 2 * (ALONG_Y - 1))], send7)
    wait_bytes(grid.at[pl.ds(0, 3)], send5)
    wait_bytes(grid.at[pl.ds(0, 4)], send6)

    @pl.when(collects)
    def _():
        wait_bytes(grid.at[r, pl.ds(0, PAIR * (OWNERS - 1))], send2)
        wait_bytes(metas.at[pl.ds(0, OWNERS - 1)], send3)
        wait_bytes(sb.at[pl.ds(0, CHUNKS - 1)], send1)
        wait_bytes(notes.at[pl.ds(0, CHUNKS - 1)], send8)

    @pl.when(jnp.logical_not(collects))
    def _():
        wait_bytes(sb, send1)
        wait_bytes(notes.at[pl.ds(0, CHUNKS)], send8)


def near(array):
    return pltpu.with_memory_space_constraint(array, pltpu.HBM)


def shards(deltas, scales, held_block, block_dest, rollout_old):
    capacity, size = rollout_old.shape[0], rollout_old.shape[1]
    count = CHUNKS * ALONG_Y
    dma, vmem = pltpu.SemaphoreType.DMA, pltpu.VMEM
    out = pl.pallas_call(
        functools.partial(kernel, capacity),
        out_shape=jax.ShapeDtypeStruct((capacity, CHUNKS, ROWS, LANES), BF16),
        in_specs=[
            pl.BlockSpec(memory_space=pltpu.HBM),
            pl.BlockSpec(memory_space=pltpu.HBM),
            pl.BlockSpec(memory_space=pltpu.HBM),
            pl.BlockSpec(memory_space=pltpu.HBM),
            pl.BlockSpec(memory_space=pltpu.HBM),
        ],
        out_specs=pl.BlockSpec(memory_space=pltpu.VMEM),
        scratch_shapes=[
            vmem((1,), BF16), pltpu.SMEM((1,), jnp.int32), pltpu.SMEM(block_dest.shape, jnp.int32),
            vmem((CHUNKS, ROWS, LANES), BF16),
            vmem((1, LANES), F32),
            vmem((count, ROWS, LANES), BF16),
            vmem((count, 1, LANES), F32),
            vmem((OWNERS, PAIR + 1, ROWS, LANES), BF16),
            vmem((CHUNKS, TILES, ROWS, LANES), BF16),
            vmem((OWNERS, ROWS, LANES), BF16),
            vmem((capacity * ROWS, 4 * LANES), BF16),
            vmem((capacity, CHUNKS, ROWS, LANES), BF16),
            dma, dma, dma((3,)),
            dma, dma,
            dma, dma((2,)),
            dma, dma((2,)),
            dma, dma((ALONG_Y,)),
            dma, dma((3,)),
            dma, dma((4,)),
            dma, dma,
            dma, dma,
            pltpu.SemaphoreType.REGULAR,
        ],
        compiler_params=pltpu.CompilerParams(
            collective_id=1, has_side_effects=True, vmem_limit_bytes=40 * 1024 * 1024
        ),
    )(
        scales,
        held_block,
        near(block_dest),
        near(deltas.reshape(CHUNKS, ROWS, LANES)),
        near(rollout_old.reshape(capacity, CHUNKS, ROWS, LANES)),
    )
    return out.reshape(capacity, size, size)


def solution(mesh):
    in_specs = (
        P(("fsdp", "expert"), None, None),
        P(("fsdp", "expert")),
        P(("fsdp", "expert")),
        P(),
        P("expert", None, None),
    )
    return jax.shard_map(shards, mesh=mesh, in_specs=in_specs, out_specs=P("expert", None, None), check_vma=False)
```

time: 51.5 us -> 49.2 us (0.955)
  Pallas kernels: 49.1 us -> 46.8 us
    pallas_call x1, Pallas kernels: 49.1 us -> 46.8 us  [shards(): pl.pallas_call(functools.partial(kernel, capacity), out_shape=jax.ShapeDt...]
where the time goes in v4:
time: 49.2 us; the launch traced here: 49.1 us
  Pallas kernels  46.8 us (95%)
  between operations  1.31 us (3%)
  local copies, waits for them, and re-layouts  0.93 us (2%)
    pallas_call x1, Pallas kernels, shards(): pl.pallas_call(functools.partial(kernel, capacity), out_shape=jax.ShapeDt...  46.8 us

profile of v4, /device:TPU:1, one launch (start us, length us, event | category | flops | bytes accessed | tf_op | source)
XLA Modules:
  0.0 49.1 jit_solution(16327300898540497775)
XLA Ops:
  1.3 46.8 %shard_map.55 = bf16[28,8,16,128]{3,2,1,0:T(8,128)(2,1)S(1)} custom-call(bf16[1]{0:T(256)(128)(2,1)S(6)} %copy.7.scale_hbm, s32[1]{0:T(128)S(6)} %copy.8.held_hbm, s32[224]{0:T(256)} %dest_hbm.1, bf16[8,16,128]{2,1,0:T(8,128)(2,1)} %bitcast.5, bf16[28,8,16,128]{3,2,1,0:T(8,128)(2,1)} %bitcast.4), custom_call_target="tpu_custom_call" | custom-call | tf_op jit(solution)/shard_map/pallas_call | solution.py:262
  48.1 0.9 %copy.9 = bf16[28,128,128]{2,1,0:T(8,128)(2,1)} copy(bf16[28,128,128]{2,1,0:T(8,128)(2,1)S(1)} %bitcast.3) | data formatting | bytes 1835008

commit v5 on v4

--- a/solution.py
+++ b/solution.py
@@ -36,8 +36,8 @@
     return jnp.where(lane == f, dest, jnp.where(lane == f + LANES // 2, scale, 0.0))
 
 
-def select_blocks(e, capacity, raw, notes, sendz):
-    count = raw.shape[0]
+def plan_blocks(e, capacity, notes, choose, sendz):
+    count = notes.shape[0]
     total = jnp.sum(notes[...], axis=0)
     scale = jnp.concatenate([total[:, LANES // 2 :], total[:, : LANES // 2]], axis=1)
     held = (iota((1, LANES), 1) < LANES // 2) & (total > 0.0)
@@ -54,11 +54,7 @@
     places = jnp.dot(jnp.broadcast_to(place, (8, LANES)).astype(BF16), spread, preferred_element_type=F32)[0:1]
     target = places.astype(jnp.int32) * ROWS + iota((1, wide), 1) % ROWS
     tall = PAIR * OWNERS * ROWS
-    choose = (iota((tall, wide), 0) == target).astype(F32).astype(BF16)
-    data = raw[...].reshape(wide, LANES)
-    chosen = jnp.dot(choose, data, preferred_element_type=F32).astype(BF16).reshape(PAIR, OWNERS, ROWS, LANES)
-    for k in range(PAIR):
-        sendz[:, k] = chosen[k]
+    choose[...] = (iota((tall, wide), 0) == target).astype(F32).astype(BF16)
     mine = iota((PAIR * OWNERS, LANES), 0).astype(F32) == place
     slots = jnp.sum(jnp.where(mine, slot, 0.0), axis=1, keepdims=True)
     scales = jnp.sum(jnp.where(mine, scale, 0.0), axis=1, keepdims=True)
@@ -79,10 +75,18 @@
         sendz[o, 2] = tile.astype(BF16)
 
 
+def move_blocks(choose, raw, sendz):
+    count = raw.shape[0]
+    data = raw[...].reshape(count * ROWS, LANES)
+    chosen = jnp.dot(choose[...], data, preferred_element_type=F32).astype(BF16).reshape(PAIR, OWNERS, ROWS, LANES)
+    for k in range(PAIR):
+        sendz[:, k] = chosen[k]
+
+
 def kernel(
     capacity, scale_hbm, held_hbm, dest_hbm, deltas_ref, old_ref, out_ref,
-    scale_ref, held_ref, dest_ref, sb, note, raw, notes, sendz, grid, metas, weights, old, in_sem, old_sem, small_sem,
-    send1, recv1, send2, recv2, send3, recv3, send4, recv4, send5, recv5, send6, recv6, send7, recv7, send8, recv8, ready,
+    scale_ref, held_ref, dest_ref, note, raw, notes, choose, sendz, grid, metas, weights, old, in_sem, old_sem, small_sem,
+    send1, recv1, send2, recv2, send3, recv3, send4, recv4, send5, recv5, send6, recv6, send7, recv7, send8, recv8, ready, go,
 ):
     f, e = lax.axis_index("fsdp"), lax.axis_index("expert")
     y, r = lax.div(f, CHUNKS), lax.rem(f, CHUNKS)
@@ -103,62 +107,63 @@
     def wait_bytes(ref, sem):
         pltpu.make_async_copy(ref, ref, sem).wait()
 
-    barrier = pltpu.get_barrier_semaphore()
-
-    def greet(to_f, to_e):
-        pl.semaphore_signal(barrier, inc=1, **where(to_f, to_e))
-
-    @pl.when(collects)
-    def _():
-        for d in range(1, count):
-            greet(lax.rem(f + d, count), e)
-        for plane in range(1, OWNERS):
-            pl.when(plane > e)(functools.partial(greet, f, plane))
-
-    for h in range(2):
-        pl.when(e < base + h)(functools.partial(greet, f, base + h))
-    for d in range(1, ALONG_Y):
-        greet(lax.rem(f + d * CHUNKS, count), e)
-    for d in range(1, 4):
-        greet(y * CHUNKS + lax.rem(r + 2 * d, CHUNKS), e)
-    sibling = y * CHUNKS + x * 2 + (1 - core)
-    greet(sibling, e)
-
-    fetch = pltpu.make_async_copy(deltas_ref, sb, in_sem)
-    fetch.start()
-    fetch_old = pltpu.make_async_copy(old_ref, old, old_sem)
-    fetch_old.start()
     small = [
         pltpu.make_async_copy(src, dst, small_sem.at[i])
         for i, (src, dst) in enumerate([(scale_hbm, scale_ref), (held_hbm, held_ref), (dest_hbm, dest_ref)])
     ]
     for copy in small:
         copy.start()
+
+    barrier = pltpu.get_barrier_semaphore()
+
+    def greet(to_f, to_e):
+        pl.semaphore_signal(barrier, inc=1, **where(to_f, to_e))
+
+    @pl.when(collects)
+    def _():
+        for d in FAR_FIRST + (0,):
+            for shift in range(d == 0, CHUNKS):
+                greet(lax.rem(y + d, ALONG_Y) * CHUNKS + lax.rem(r + shift, CHUNKS), e)
+        for plane in range(1, OWNERS):
+            pl.when(plane > e)(functools.partial(greet, f, plane))
+
+    sibling = y * CHUNKS + x * 2 + (1 - core)
+
+    for h in range(2):
+        pl.when(e < base + h)(functools.partial(greet, f, base + h))
+
     for copy in small:
         copy.wait()
     note[...] = own_meta(f, scale_ref, held_ref, dest_ref)
-    fetch.wait()
 
     lower = (base < e).astype(jnp.int32) + (base + 1 < e).astype(jnp.int32)
-    pl.semaphore_wait(barrier, ALONG_Y + 3 + lower + jnp.where(collects, CHUNKS - 1 + e, CHUNKS))
+    pl.semaphore_wait(barrier, lower + jnp.where(collects, CHUNKS - 1 + e, CHUNKS))
     for h in range(2):
         def answer(h=h):
             pl.semaphore_signal(ready, inc=1, **where(f, base + h))
         pl.when(base + h < e)(answer)
 
     for i in range(CHUNKS):
+        def send_note(i=i):
+            remote(note, notes.at[f], send8, recv8, home(e) * CHUNKS + i, e).start()
+        pl.when(jnp.logical_not(collects & (r == i)))(send_note)
+    for i in range(CHUNKS):
         def send_chunk(i=i):
-            remote(sb.at[i], raw.at[f], send1, recv1, home(e) * CHUNKS + i, e).start()
-            remote(note, notes.at[f], send8, recv8, home(e) * CHUNKS + i, e).start()
+            remote(deltas_ref.at[i], raw.at[f], send1, recv1, home(e) * CHUNKS + i, e).start()
         pl.when(jnp.logical_not(collects & (r == i)))(send_chunk)
+    fetch_old = pltpu.make_async_copy(old_ref, old, old_sem)
+    fetch_old.start()
 
     @pl.when(collects)
     def _():
-        raw[f] = sb[r]
+        own_chunk = pltpu.make_async_copy(deltas_ref.at[r], raw.at[f], in_sem)
+        own_chunk.start()
         notes[f] = note[...]
+        own_chunk.wait()
+        wait_bytes(notes.at[pl.ds(0, count - 1)], recv8)
+        plan_blocks(e, capacity, notes, choose, sendz)
         wait_bytes(raw.at[pl.ds(0, count - 1)], recv1)
-        wait_bytes(notes.at[pl.ds(0, count - 1)], recv8)
-        select_blocks(e, capacity, raw, notes, sendz)
+        move_blocks(choose, raw, sendz)
         mine = pl.ds(y * PIECE + half * PAIR, PAIR)
         place = y * 2 + half
 
@@ -170,9 +175,13 @@
             pl.when(plane < e)(functools.partial(along_z, plane))
         grid[r, mine] = sendz[e, pl.ds(0, PAIR)]
         metas[place] = sendz[e, PAIR]
+        for d in FAR_FIRST:
+            pl.semaphore_signal(go, inc=1, **where(lax.rem(f + d * CHUNKS, count), e))
         pl.when(e < OWNERS - 1)(lambda: pl.semaphore_wait(ready, OWNERS - 1 - e))
         for plane in range(1, OWNERS):
             pl.when(plane > e)(functools.partial(along_z, plane))
+
+    pl.when(jnp.logical_not(collects))(lambda: pl.semaphore_wait(go, 1))
 
     def along_x(row):
         part = grid.at[r, pl.ds(row * PIECE, PIECE)]
@@ -242,12 +251,12 @@
     def _():
         wait_bytes(grid.at[r, pl.ds(0, PAIR * (OWNERS - 1))], send2)
         wait_bytes(metas.at[pl.ds(0, OWNERS - 1)], send3)
-        wait_bytes(sb.at[pl.ds(0, CHUNKS - 1)], send1)
+        wait_bytes(raw.at[pl.ds(0, CHUNKS - 1)], send1)
         wait_bytes(notes.at[pl.ds(0, CHUNKS - 1)], send8)
 
     @pl.when(jnp.logical_not(collects))
     def _():
-        wait_bytes(sb, send1)
+        wait_bytes(raw.at[pl.ds(0, CHUNKS)], send1)
         wait_bytes(notes.at[pl.ds(0, CHUNKS)], send8)
 
 
@@ -272,10 +281,10 @@
         out_specs=pl.BlockSpec(memory_space=pltpu.VMEM),
         scratch_shapes=[
             vmem((1,), BF16), pltpu.SMEM((1,), jnp.int32), pltpu.SMEM(block_dest.shape, jnp.int32),
-            vmem((CHUNKS, ROWS, LANES), BF16),
             vmem((1, LANES), F32),
             vmem((count, ROWS, LANES), BF16),
             vmem((count, 1, LANES), F32),
+            vmem((PAIR * OWNERS * ROWS, count * ROWS), BF16),
             vmem((OWNERS, PAIR + 1, ROWS, LANES), BF16),
             vmem((CHUNKS, TILES, ROWS, LANES), BF16),
             vmem((OWNERS, ROWS, LANES), BF16),
@@ -291,6 +300,7 @@
             dma, dma,
             dma, dma,
             pltpu.SemaphoreType.REGULAR,
+            pltpu.SemaphoreType.REGULAR,
         ],
         compiler_params=pltpu.CompilerParams(
             collective_id=1, has_side_effects=True, vmem_limit_bytes=40 * 1024 * 1024

time: 49.2 us -> 48.7 us (0.990)
  Pallas kernels: 46.8 us -> 46.3 us
where the time goes in v5:
time: 48.7 us; the launch traced here: 48.6 us
  Pallas kernels  46.3 us (95%)
  between operations  1.31 us (3%)
  local copies, waits for them, and re-layouts  0.93 us (2%)
    pallas_call x1, Pallas kernels, shards(): pl.pallas_call(functools.partial(kernel, capacity), out_shape=jax.ShapeDt...  46.3 us

profile of v5, /device:TPU:1, one launch (start us, length us, event | category | flops | bytes accessed | tf_op | source)
XLA Modules:
  0.0 48.6 jit_solution(9735472656666203439)
XLA Ops:
  1.3 46.3 %shard_map.55 = bf16[28,8,16,128]{3,2,1,0:T(8,128)(2,1)S(1)} custom-call(bf16[1]{0:T(256)(128)(2,1)S(6)} %copy.7.scale_hbm, s32[1]{0:T(128)S(6)} %copy.8.held_hbm, s32[224]{0:T(256)} %dest_hbm.1, bf16[8,16,128]{2,1,0:T(8,128)(2,1)} %bitcast.5, bf16[28,8,16,128]{3,2,1,0:T(8,128)(2,1)} %bitcast.4), custom_call_target="tpu_custom_call" | custom-call | tf_op jit(solution)/shard_map/pallas_call | solution.py:271
  47.6 0.9 %copy.9 = bf16[28,128,128]{2,1,0:T(8,128)(2,1)} copy(bf16[28,128,128]{2,1,0:T(8,128)(2,1)S(1)} %bitcast.3) | data formatting | bytes 1835008

commit v6 on v5

--- a/solution.py
+++ b/solution.py
@@ -143,14 +143,18 @@
             pl.semaphore_signal(ready, inc=1, **where(f, base + h))
         pl.when(base + h < e)(answer)
 
-    for i in range(CHUNKS):
+    for shift in FAR_FIRST + (0,):
+        i = lax.rem(r + shift, CHUNKS)
+
         def send_note(i=i):
             remote(note, notes.at[f], send8, recv8, home(e) * CHUNKS + i, e).start()
-        pl.when(jnp.logical_not(collects & (r == i)))(send_note)
-    for i in range(CHUNKS):
+        pl.when(jnp.logical_not(collects))(send_note) if shift == 0 else send_note()
+    for shift in FAR_FIRST + (0,):
+        i = lax.rem(r + shift, CHUNKS)
+
         def send_chunk(i=i):
             remote(deltas_ref.at[i], raw.at[f], send1, recv1, home(e) * CHUNKS + i, e).start()
-        pl.when(jnp.logical_not(collects & (r == i)))(send_chunk)
+        pl.when(jnp.logical_not(collects))(send_chunk) if shift == 0 else send_chunk()
     fetch_old = pltpu.make_async_copy(old_ref, old, old_sem)
     fetch_old.start()
 
@@ -208,10 +212,10 @@
         pl.when(y != row)(arrive)
 
     pl.when(y >= 4)(own_piece)
-    for row in range(4, 8):
+    for row in (5, 4, 6):
         other_piece(row)
     pl.when(y < 4)(own_piece)
-    for row in range(4):
+    for row in (7, 0, 1, 2, 3):
         other_piece(row)
 
     remote(grid.at[r], grid.at[r], send6, recv6.at[0], sibling, e).start()
@@ -231,11 +235,12 @@
         new = old[:, i].astype(F32) + update.reshape(capacity, ROWS, LANES)
         out_ref[:, i] = new.astype(BF16)
 
+    add(r)
     for d in (1, 3, 2):
         src = lax.rem(r + CHUNKS - 2 * d, CHUNKS)
         wait_bytes(grid.at[src], recv5.at[d - 1])
         remote(grid.at[src], grid.at[src], send6, recv6.at[d], sibling, e).start()
-    for d in range(4):
+    for d in (1, 3, 2):
         add(lax.rem(r + CHUNKS - 2 * d, CHUNKS))
     for d in (0, 1, 3, 2):
         src = lax.rem(r + CHUNKS - 2 * d, CHUNKS) + 1 - 2 * core

time: 48.7 us -> 48.6 us (level)
  no operation moved by 1% of the time
where the time goes in v6:
time: 48.6 us; the launch traced here: 48.5 us
  Pallas kernels  46.2 us (95%)
  between operations  1.31 us (3%)
  local copies, waits for them, and re-layouts  0.93 us (2%)
    pallas_call x1, Pallas kernels, shards(): pl.pallas_call(functools.partial(kernel, capacity), out_shape=jax.ShapeDt...  46.2 us

profile of v6, /device:TPU:1, one launch (start us, length us, event | category | flops | bytes accessed | tf_op | source)
XLA Modules:
  0.0 48.5 jit_solution(16705788629576202394)
XLA Ops:
  1.3 46.2 %shard_map.55 = bf16[28,8,16,128]{3,2,1,0:T(8,128)(2,1)S(1)} custom-call(bf16[1]{0:T(256)(128)(2,1)S(6)} %copy.7.scale_hbm, s32[1]{0:T(128)S(6)} %copy.8.held_hbm, s32[224]{0:T(256)} %dest_hbm.1, bf16[8,16,128]{2,1,0:T(8,128)(2,1)} %bitcast.5, bf16[28,8,16,128]{3,2,1,0:T(8,128)(2,1)} %bitcast.4), custom_call_target="tpu_custom_call" | custom-call | tf_op jit(solution)/shard_map/pallas_call | solution.py:276
  47.5 0.9 %copy.9 = bf16[28,128,128]{2,1,0:T(8,128)(2,1)} copy(bf16[28,128,128]{2,1,0:T(8,128)(2,1)S(1)} %bitcast.3) | data formatting | bytes 1835008

commit v7 on v6

--- a/solution.py
+++ b/solution.py
@@ -21,7 +21,8 @@
 
 
 def home(e):
-    return lax.rem(lax.div(e, 2) + 4, ALONG_Y)
+    pair = lax.div(e, 2)
+    return jnp.where(pair < 4, pair + 3, jnp.where(pair < 7, pair - 4, 7))
 
 
 def iota(shape, dim):
@@ -93,7 +94,8 @@
     x, core = lax.div(r, 2), lax.rem(r, 2)
     half = lax.rem(e, 2)
     collects = y == home(e)
-    base = lax.rem(y + 4, ALONG_Y) * 2
+    base = 2 * jnp.where(y < 3, y + 4, jnp.where(y < 7, y - 3, 7))
+    early = (y >= 3) & (y < 7)
     count = CHUNKS * ALONG_Y
 
     def where(to_f, to_e):
@@ -211,11 +213,11 @@
             along_x(row)
         pl.when(y != row)(arrive)
 
-    pl.when(y >= 4)(own_piece)
-    for row in (5, 4, 6):
+    pl.when(early)(own_piece)
+    for row in (4, 3, 5):
         other_piece(row)
-    pl.when(y < 4)(own_piece)
-    for row in (7, 0, 1, 2, 3):
+    pl.when(jnp.logical_not(early))(own_piece)
+    for row in (6, 0, 1, 2, 7):
         other_piece(row)
 
     remote(grid.at[r], grid.at[r], send6, recv6.at[0], sibling, e).start()

time: 48.6 us -> 47.8 us (0.984)
  Pallas kernels: 46.2 us -> 45.4 us
    pallas_call x1, Pallas kernels: 46.2 us -> 45.4 us  [shards(): pl.pallas_call(functools.partial(kernel, capacity), out_shape=jax.ShapeDt...]
where the time goes in v7:
time: 47.8 us; the launch traced here: 47.6 us
  Pallas kernels  45.4 us (95%)
  between operations  1.31 us (3%)
  local copies, waits for them, and re-layouts  0.93 us (2%)
    pallas_call x1, Pallas kernels, shards(): pl.pallas_call(functools.partial(kernel, capacity), out_shape=jax.ShapeDt...  45.4 us

profile of v7, /device:TPU:1, one launch (start us, length us, event | category | flops | bytes accessed | tf_op | source)
XLA Modules:
  0.0 47.6 jit_solution(3418916947564528420)
XLA Ops:
  1.3 45.4 %shard_map.55 = bf16[28,8,16,128]{3,2,1,0:T(8,128)(2,1)S(1)} custom-call(bf16[1]{0:T(256)(128)(2,1)S(6)} %copy.7.scale_hbm, s32[1]{0:T(128)S(6)} %copy.8.held_hbm, s32[224]{0:T(256)} %dest_hbm.1, bf16[8,16,128]{2,1,0:T(8,128)(2,1)} %bitcast.5, bf16[28,8,16,128]{3,2,1,0:T(8,128)(2,1)} %bitcast.4), custom_call_target="tpu_custom_call" | custom-call | tf_op jit(solution)/shard_map/pallas_call | solution.py:278
  46.7 0.9 %copy.9 = bf16[28,128,128]{2,1,0:T(8,128)(2,1)} copy(bf16[28,128,128]{2,1,0:T(8,128)(2,1)S(1)} %bitcast.3) | data formatting | bytes 1835008
